TPU v7x, 256 devices: a whole 4x4x8 slice. The times are simulated.
256 devices in a mesh: layer: 8 (over x, y_hi), group: 32 (over z, y_lo, core).
Axes of the slice: x: 4, y: 4 (y_hi: 2, y_lo: 2; y = y_hi * 2 + y_lo), z: 8, core: 2. Of those that a mesh axis runs over, the one named last changes fastest.
Arguments:
- activations: bfloat16 [16, 64, 64, 4096], P('layer', 'group'), may hold values from -6 to 6
- out_grads: bfloat16 [16, 64, 64, 4096], P('layer', 'group'), may hold values from -0.09375 to 0.09375
- in_factor: bfloat16 [16, 4096, 32], P('layer'), may hold values from -0.09375 to 0.09375
- out_factor: bfloat16 [16, 4096, 32], P('layer'), may hold values from -0.09375 to 0.09375
- stored_rows: bfloat16 [32768, 16, 1024], P('group', 'layer'), may hold values from -0.5390625 to 0.5390625
- example_class: int32 [64], P('group'), may hold values from 0 to 31
Outputs:
- self_gram: bfloat16 [32, 1024, 1024], P('group', 'layer')
- cross_gram: bfloat16 [32, 2, 1024, 1024], P('group', None, 'layer')
- class_scores: bfloat16 [32, 32768], P('layer', 'group')
All inputs are finite; a program needn't handle non-finite values.
Results may differ from a plain program's by a relative error of at most 0.023.
Values may be sent and summed in bfloat16 or wider, within the bound.
A program may use at most 64 MiB of HBM per device.

v0:
```python
import jax
import jax.numpy as jnp
from jax import lax
from jax.sharding import PartitionSpec as P

CLASSES = 32


def from_behind(shard, axis, by):
    peers = lax.axis_size(axis)
    return lax.ppermute(shard, axis, [(i, (i + by) % peers) for i in range(peers)])


def inner_block(left_rows, right_rows):
    return lax.dot_general(
        left_rows, right_rows, (((1,), (1,)), ((), ())), preferred_element_type=jnp.float32
    )


def per_device(activations, out_grads, in_factor, out_factor, stored_rows, example_class):
    layer_count = activations.shape[0]
    example_count = activations.shape[1]
    token_count = activations.shape[2]
    model_width = activations.shape[3]
    factor_rank = in_factor.shape[2]
    pieces = []
    for layer_index in range(layer_count):
        left_side = jnp.dot(
            activations[layer_index].reshape(-1, model_width),
            in_factor[layer_index],
            preferred_element_type=jnp.float32,
        ).reshape(example_count, token_count, factor_rank)
        right_side = jnp.dot(
            out_grads[layer_index].reshape(-1, model_width),
            out_factor[layer_index],
            preferred_element_type=jnp.float32,
        ).reshape(example_count, token_count, factor_rank)
        outer = jnp.einsum("etp,etq->epq", left_side, right_side, precision=lax.Precision.HIGHEST)
        pieces.append(outer.reshape(example_count, factor_rank * factor_rank))
    fresh = jnp.concatenate(pieces, axis=1)
    one_hot = (example_class[:, None] == jnp.arange(CLASSES, dtype=jnp.int32)[None, :]).astype(
        jnp.float32
    )
    local_sums = jnp.dot(
        one_hot.T, fresh, precision=lax.Precision.HIGHEST, preferred_element_type=jnp.float32
    )
    class_sums = lax.psum(local_sums.astype(jnp.bfloat16), "group")
    row_count = stored_rows.shape[0]
    own_block = stored_rows.reshape(row_count, -1)
    near_block = from_behind(own_block, "group", -1)
    far_block = from_behind(near_block, "group", -1)
    score_part = inner_block(class_sums, own_block)
    tiles = jnp.stack(
        [
            inner_block(own_block, own_block),
            inner_block(own_block, near_block),
            inner_block(own_block, far_block),
        ]
    )
    tile_sums, score_sums = (
        lax.psum_scatter(
            tiles.astype(jnp.bfloat16), "layer", scatter_dimension=1, tiled=True
        ).astype(jnp.float32),
        lax.psum_scatter(
            score_part[None].astype(jnp.bfloat16), "layer", scatter_dimension=1, tiled=True
        ).astype(jnp.float32),
    )
    score_sums = score_sums[0]
    tile_out = tile_sums.astype(jnp.bfloat16)
    return (tile_out[0][None], tile_out[1:][None], score_sums.astype(jnp.bfloat16))


def solution(mesh):
    placed = (
        P("layer", "group", None, None),
        P("layer", "group", None, None),
        P("layer", None, None),
        P("layer", None, None),
        P("group", "layer", None),
        P("group"),
    )
    return jax.shard_map(
        per_device,
        mesh=mesh,
        in_specs=placed,
        out_specs=(P("group", "layer", None), P("group", None, "layer", None), P("layer", "group")),
        check_vma=False,
    )
```

profile of v0, /device:TPU:1, one launch (start us, length us, event | category | flops | bytes accessed | tf_op | source)
XLA Modules:
  0.0 503.1 jit_solution(6720145069418714995)
XLA Ops:
  7.2 0.0 all-reduce.4.cloned.1.call-start
  7.3 3.8 copy.15
  11.1 1.9 copy-done
  13.0 3.2 collective-permute-start
  16.2 45.7 %collective-permute-done = bf16[1024,2048]{1,0:T(8,128)(2,1)} collective-permute-done((bf16[1024,2048]{1,0:T(8,128)(2,1)S(1)}, bf16[1024,2048]{1,0:T(8,128)(2,1)}, u32[]{:S(2)}, u32[]{:S(2)}) %collective-permute-start) | collective-permute-done | bytes 4194336 | tf_op jit(solution)/shard_map/ppermute | solution.py:11
  62.0 4.9 collective-permute-start.1
  66.9 0.6 fusion.10
  67.4 0.0 copy-done.4
  67.5 0.6 fusion.12
  68.0 0.2 fusion.33
  68.2 0.1 reshape.31
  68.3 0.6 fusion.6
  68.9 1.8 fusion.8
  70.7 0.2 fusion.34
  70.9 0.1 reshape.32
  71.0 1.1 convolution_convert_fusion
  72.1 0.0 all-reduce.4.cloned.1.call-update
  72.1 0.0 all-reduce.6.cloned.1.call-start
  72.2 8.0 %fusion.2 = bf16[1,1024,1024]{2,1,0:T(8,128)(2,1)S(1)} fusion(bf16[1024,2,1024]{2,1,0:T(2,128)(2,1)} %param.10), kind=kOutput, calls=%fused_computation.5 | convolution fusion | flops 4296015872 | bytes 6291456 | tf_op jit(solution)/shard_map/dot_general | solution.py:15
  80.2 214.5 %all-reduce.4.cloned.1.call-done = bf16[32,2048]{1,0:T(8,128)(2,1)} async-done(((bf16[32,2048]{1,0:T(8,128)(2,1)}), bf16[32,2048]{1,0:T(8,128)(2,1)}) %all-reduce.4.cloned.1.call-update) | async-done | bytes 131088 | tf_op jit(solution)/shard_map/psum | solution.py:47
  294.7 4.2 fusion.5
  298.9 0.2 reduce-scatter.3.cloned.1.call-start
  299.2 8.1 %convert_bitcast_fusion.1 = bf16[1,1024,1024]{2,1,0:T(8,128)(2,1)S(1)} fusion(bf16[1024,2048]{1,0:T(8,128)(2,1)} %bitcast.61, bf16[1024,2048]{1,0:T(8,128)(2,1)} %collective-permute-done), kind=kOutput, calls=%fused_computation.7 | convolution fusion | flops 4296015872 | bytes 10485760 | tf_op jit(solution)/shard_map/dot_general | solution.py:15
  307.3 7.0 %convert_bitcast_fusion = bf16[1,1024,1024]{2,1,0:T(8,128)(2,1)S(1)} fusion(bf16[1024,2048]{1,0:T(8,128)(2,1)S(1)} %bitcast.62, bf16[1024,2048]{1,0:T(8,128)(2,1)} %collective-permute-done.1), kind=kOutput, calls=%fused_computation.6 | convolution fusion | flops 4296015872 | bytes 10485760 | tf_op jit(solution)/shard_map/dot_general | solution.py:15
  314.3 3.1 pad_maximum_fusion
  317.4 0.6 copy-done.7
  318.1 0.6 dynamic-slice
  319.3 62.9 %all-reduce.6.cloned.1.call-done = bf16[1,32,1024]{2,1,0:T(8,128)(2,1)} async-done(((bf16[1,32,1024]{2,1,0:T(8,128)(2,1)}), bf16[1,32,1024]{2,1,0:T(8,128)(2,1)}) %all-reduce.6.cloned.1.call-update) | async-done | bytes 65552
  382.2 1.3 dynamic-slice_bitcast_fusion
  383.6 109.5 %reduce-scatter.3.cloned.1.call-done = bf16[3,128,1024]{2,1,0:T(8,128)(2,1)} async-done(((bf16[3,1024,1024]{2,1,0:T(8,128)(2,1)}), bf16[3,128,1024]{2,1,0:T(8,128)(2,1)}) %reduce-scatter.3.cloned.1.call-update) | async-done | bytes 786448 | tf_op jit(solution)/shard_map/reduce_scatter | solution.py:61
  493.1 1.9 slice_bitcast_fusion
  494.9 1.7 slice.40
  (16 shorter events, 0.1 us)
Async XLA Ops:
  7.2 287.5 %all-reduce.4.cloned.1.call-start = ((), (), s32[]{:S(2)}) async-start(), calls=%async_computation.2 | async-start | bytes 262144 | tf_op jit(solution)/shard_map/psum | solution.py:47
  7.2 59.6 %copy-start.3 = (bf16[2,2,64,4096]{3,2,1,0:T(8,128)(2,1)S(1)}, bf16[2,2,64,4096]{3,2,1,0:T(8,128)(2,1)}, u32[]{:S(2)}) copy-start(bf16[2,2,64,4096]{3,2,1,0:T(8,128)(2,1)} %param.7) | copy-start | bytes 6291460
  7.2 59.6 %copy-start.5 = (bf16[2,4096,32]{1,2,0:T(8,128)(2,1)S(1)}, bf16[2,4096,32]{1,2,0:T(8,128)(2,1)}, u32[]{:S(2)}) copy-start(bf16[2,4096,32]{1,2,0:T(8,128)(2,1)} %param.9) | copy-start | bytes 1572868
  7.2 60.2 %copy-start.4 = (bf16[2,2,64,4096]{3,2,1,0:T(8,128)(2,1)S(1)}, bf16[2,2,64,4096]{3,2,1,0:T(8,128)(2,1)}, u32[]{:S(2)}) copy-start(bf16[2,2,64,4096]{3,2,1,0:T(8,128)(2,1)} %param.6) | copy-start | bytes 6291460
  7.2 60.2 %copy-start.6 = (bf16[2,4096,32]{1,2,0:T(8,128)(2,1)S(1)}, bf16[2,4096,32]{1,2,0:T(8,128)(2,1)}, u32[]{:S(2)}) copy-start(bf16[2,4096,32]{1,2,0:T(8,128)(2,1)} %param.8) | copy-start | bytes 1572868
  11.1 1.9 copy-start
  11.1 60.0 %copy-start.2 = (s32[2]{0:T(128)S(1)}, s32[2]{0:T(128)}, u32[]{:S(2)}) copy-start(s32[2]{0:T(128)} %param.11) | copy-start | bytes 28
  13.0 49.0 %collective-permute-start = (bf16[1024,2048]{1,0:T(8,128)(2,1)S(1)}, bf16[1024,2048]{1,0:T(8,128)(2,1)}, u32[]{:S(2)}, u32[]{:S(2)}) collective-permute-start(bf16[1024,2048]{1,0:T(8,128)(2,1)S(1)} %bitcast.59), channel_id=1, source_target_pairs={{0,31},{1,0},{2,1},{3,2},{4,3},{5,4},{6,5},{7,6},{8,7},{9,8},{10,9... | collective-permute-start | bytes 12582920 | tf_op jit(solution)/shard_map/ppermute | solution.py:11
  62.0 245.3 %collective-permute-start.1 = (bf16[1024,2048]{1,0:T(8,128)(2,1)}, bf16[1024,2048]{1,0:T(8,128)(2,1)}, u32[]{:S(2)}, u32[]{:S(2)}) collective-permute-start(bf16[1024,2048]{1,0:T(8,128)(2,1)} %collective-permute-done), channel_id=1, source_target_pairs={{0,31},{1,0},{2,1},{3,2},{4,3},{5,4},{6,5},{7,6},{8,7},{9,8},{10,9... | collective-permute-start | bytes 12582920 | tf_op jit(solution)/shard_map/ppermute | solution.py:11
  72.1 310.1 %all-reduce.6.cloned.1.call-start = ((), (), s32[]{:S(2)}) async-start(), calls=%async_computation.3 | async-start | bytes 131072
  298.9 194.1 %reduce-scatter.3.cloned.1.call-start = ((), (), s32[]{:S(2)}) async-start(), calls=%async_computation.1 | async-start | bytes 7077888 | tf_op jit(solution)/shard_map/reduce_scatter | solution.py:61
  299.2 8.1 %copy-start.1 = (bf16[128,8,2,1024]{3,1,2,0:T(8,128)(2,1)S(1)}, bf16[128,8,2,1024]{3,1,2,0:T(8,128)(2,1)}, u32[]{:S(2)}) copy-start(bf16[128,8,2,1024]{3,1,2,0:T(8,128)(2,1)} %copy-done) | copy-start | bytes 12582916
  317.4 0.7 copy-start.7
Sparse Core Ops, SparseCore 0:
  72.2 222.3 all-reduce.3
  299.1 83.1 all-reduce.5
  386.4 106.5 reduce-scatter.2
where the time goes:
time: 503 us
  waiting for transfers between devices  433 us (86%)
  matrix products  32.3 us (6%)
  between operations  14.6 us (3%)
  local copies, waits for them, and re-layouts  12.1 us (2%)
  starting transfers between devices  8.4 us (2%)
    psum x1, waiting for transfers between devices, per_device(): class_sums = lax.psum(local_sums.astype(jnp.bfloat16), 'group')  214 us
    reduce_scatter x1, waiting for transfers between devices, per_device(): lax.psum_scatter(tiles.astype(jnp.bfloat16), 'layer', scatter_dimension=1...  109 us
    unnamed x4, waiting for transfers between devices  63 us
    ppermute x2, waiting for transfers between devices, from_behind(): lax.ppermute(shard, axis, [(i, (i + by) % peers) for i in range(peers)])  45.7 us
    dot_general x4, matrix products, inner_block(): lax.dot_general(left_rows, right_rows, (((1,), (1,)), ((), ())), preferre...  27.3 us
  transfers between devices with their start and end apart: 5, of which 4 were waited for; matrix products, arithmetic and copies ran while one was open for 7% of the time, Pallas kernels for 0%

commit v1 on v0

v1 whole, which is shorter than its diff:
```python
import functools

import jax
import jax.numpy as jnp
from jax import lax
from jax.experimental import pallas as pl
from jax.experimental.pallas import tpu as pltpu
from jax.sharding import PartitionSpec as P

CLASSES = 32
MESH = pl.DeviceIdType.MESH
OWN, MATE, INNER, ALONG, CROSS = 0, 4, 8, 10, 12
PIECES = 9


def inner_block(left_rows, right_rows):
    return lax.dot_general(
        left_rows, right_rows, (((1,), (1,)), ((), ())), preferred_element_type=jnp.float32
    )


def tiles_kernel(
    own_hbm, self_ref, cross_ref,
    chunks, parts, hop, near_in, summed, home_self, home_near, home_far,
    own_sem, mate_s, mate_r, inner_s, inner_r, along_s, along_r, cross_s, cross_r,
    hop_s, hop_r, fold_s, fold_r, home_s, self_r, near_r, far_r,
):
    layer = lax.axis_index("layer")
    group = lax.axis_index("group")
    x, yh = layer // 2, layer % 2
    z, yl, core = group // 4, (group // 2) % 2, group % 2
    other = 1 - yh

    def at(xx, hh, gg):
        return (lax.rem(xx + 4, 4) * 2 + hh, lax.rem(gg + 32, 32))

    right, left = at(x + 1, yh, group), at(x - 1, yh, group)
    mirror = at(x, other, group)
    mate = at(x, yh, group + 1 - 2 * core)
    across = at(x, yh, group + 2 - 4 * yl)
    onward = at(x, yh, group + 4 - 8 * yl)
    greeted = [right, left, mirror]
    for step in (1, -1, 2, -2):
        greeted += [at(x, yh, group + step), at(x, other, group + step)]
    greeted += [at(x, yh, group + 4), at(x, yh, group - 4)]
    barrier = pltpu.get_barrier_semaphore()
    for who in greeted:
        pl.semaphore_signal(barrier, inc=1, device_id=who, device_id_type=MESH)
    own_copies = [
        pltpu.make_async_copy(own_hbm.at[k], chunks.at[pl.ds(OWN + 2 * k, 2)], own_sem.at[k])
        for k in range(2)
    ]
    for copy in own_copies:
        copy.start()
    pl.semaphore_wait(barrier, len(greeted))

    def remote(src, dst, send, recv, who):
        return pltpu.make_async_remote_copy(
            src_ref=src, dst_ref=dst, send_sem=send, recv_sem=recv, device_id=who, device_id_type=MESH
        )

    def rows_of(step):
        return step // 4, pl.ds((step % 4) * 128, 128)

    def inner_copy(step):
        k, rows = rows_of(step)
        return remote(own_hbm.at[k, yl, rows], chunks.at[INNER + k, rows], inner_s.at[step], inner_r.at[step], across)

    def along_copy(step):
        k, rows = rows_of(step)
        return remote(
            chunks.at[INNER + k, rows], chunks.at[ALONG + k, rows], along_s.at[step], along_r.at[step], onward
        )

    def mate_copy(k):
        return remote(own_hbm.at[k], chunks.at[pl.ds(MATE + 2 * k, 2)], mate_s.at[k], mate_r.at[k], mate)

    passes_inner = yl == core
    passed = jnp.where(passes_inner, INNER, ALONG)

    def cross_copy(k):
        return remote(chunks.at[passed + k], chunks.at[CROSS + k], cross_s.at[k], cross_r.at[k], mate)

    def hop_copy(p, side):
        return remote(
            parts.at[p, lax.rem(x + 2, 4), side], hop.at[p, side], hop_s.at[p, side], hop_r.at[p, side],
            right if side == 0 else left,
        )

    def fold_copy(p, side):
        to = lax.rem(x + 1, 4) if side == 0 else lax.rem(x + 3, 4)
        return remote(
            parts.at[p, to], near_in.at[p, side], fold_s.at[p, side], fold_r.at[p, side],
            right if side == 0 else left,
        )

    for step in range(8):
        inner_copy(step).start()
    mate_copy(0).start()

    @pl.when(core == 0)
    def _():
        mate_copy(1).start()

    def compute(p, left_slots, right_slots):
        for i in range(2):
            lefts, rights = left_slots(i), right_slots(i)

            def columns(n, carry):
                cols = pl.ds(pl.multiple_of(n * 256, 256), 256)
                total = None
                for a, b in zip(lefts, rights):
                    term = inner_block(chunks[a], chunks[b, cols, :])
                    total = term if total is None else total + term
                parts[p, :, i, :, cols] = total.astype(jnp.bfloat16).reshape(4, 128, 256)
                return carry

            lax.fori_loop(0, 2, columns, 0)
        for side in range(2):
            hop_copy(p, side).start()

    half = 1 - yl

    def half_piece(p, slot, is_row):
        def lefts(i):
            return [jnp.where(is_row, slot, OWN + 2 * i + half)]

        def rights(i):
            return [jnp.where(is_row, OWN + 2 * i + half, slot)]

        compute(p, lefts, rights)

    def fold(p):
        for side in range(2):
            to = lax.rem(x + 1, 4) if side == 0 else lax.rem(x + 3, 4)
            hop_copy(p, side).wait_recv()
            parts[p, to, side] = (
                parts[p, to, side].astype(jnp.float32) + hop[p, side].astype(jnp.float32)
            ).astype(jnp.bfloat16)
            fold_copy(p, side).start()

    def total_of(p):
        for side in range(2):
            fold_copy(p, side).wait_recv()
        summed[p] = (
            parts[p, x].astype(jnp.float32)
            + near_in[p, 0].astype(jnp.float32)
            + near_in[p, 1].astype(jnp.float32)
        ).astype(jnp.bfloat16)

    def self_home(k):
        return remote(summed.at[k, other], home_self.at[k], home_s.at[k, 0], self_r.at[k], mirror)

    def within_mirror():
        return remote(summed.at[2, other], home_near.at[0, 0], home_s.at[2, 0], near_r.at[0, 0], mirror)

    def within_mate():
        return remote(summed.at[2, yh], home_near.at[1, 1], home_s.at[2, 0], near_r.at[1, 1], mate)

    def within_mate_mirror():
        return remote(
            summed.at[2, other], home_near.at[2, 1], home_s.at[2, 1], near_r.at[2, 1],
            at(x, other, group + 1 - 2 * core),
        )

    def col_home(p, k, box, sems):
        return remote(summed.at[p, other], box.at[0, k], home_s.at[p, 0], sems.at[0, k], mirror)

    def row_home(p, k, box, sems, back):
        place = jnp.where(yh == k, 1, 2)
        return remote(summed.at[p], box.at[place], home_s.at[p, 0], sems.at[place, 0], at(x, k, group - back))

    def home_op(p, op):
        if p < 2:
            op(self_home(p))
        elif p == 2:

            @pl.when(core == 0)
            def _():
                op(within_mirror())

            @pl.when(core == 1)
            def _():
                op(within_mate())
                op(within_mate_mirror())
        else:
            k = (p - 3) % 2
            is_row = {0: yl == 1, 1: yl == 0, 2: core == 0}[(p - 3) // 2]
            box, sems, back = (home_far, far_r, 2) if p < 7 else (home_near, near_r, 1)

            @pl.when(is_row)
            def _():
                op(row_home(p, k, box, sems, back))

            @pl.when(jnp.logical_not(is_row))
            def _():
                op(col_home(p, k, box, sems))

    def finish(p):
        total_of(p)
        home_op(p, lambda copy: copy.start())

    def pass_on(step):
        inner_copy(step).wait_recv()
        along_copy(step).start()

    def take_along(k):
        for step in range(4 * k, 4 * k + 4):
            along_copy(step).wait_recv()

    def cross_inner(k):
        @pl.when(passes_inner)
        def _():
            cross_copy(k).start()

    def cross_along(k):
        @pl.when(jnp.logical_not(passes_inner))
        def _():
            cross_copy(k).start()

    def piece_inner(k):
        half_piece(3 + k, INNER + k, yl == 1)

    def piece_along(k):
        half_piece(5 + k, ALONG + k, yl == 0)

    def piece_cross(k):
        cross_copy(k).wait_recv()
        half_piece(7 + k, CROSS + k, core == 0)

    for copy in own_copies:
        copy.wait()
    for k in range(2):
        compute(k, lambda i: [OWN + 2 * i, OWN + 2 * i + 1], lambda i: [OWN + 2 * k, OWN + 2 * k + 1])
    pass_on(0)
    fold(0)
    mate_copy(0).wait_recv()

    @pl.when(core == 1)
    def _():
        mate_copy(1).wait_recv()

    theirs = jnp.where(core == 0, MATE, OWN + 2)
    compute(
        2,
        lambda i: [MATE * core + 2 * i, MATE * core + 2 * i + 1],
        lambda i: [theirs, theirs + 1],
    )
    fold(1)
    pass_on(1)
    finish(0)
    pass_on(2)
    fold(2)
    pass_on(3)
    cross_inner(0)
    piece_inner(0)
    finish(1)
    take_along(0)
    cross_along(0)
    piece_along(0)
    pass_on(4)
    fold(3)
    piece_cross(0)
    finish(2)
    pass_on(5)
    fold(5)
    fold(7)
    pass_on(6)
    finish(3)
    pass_on(7)
    cross_inner(1)
    piece_inner(1)
    finish(5)
    take_along(1)
    cross_along(1)
    piece_along(1)
    fold(4)
    piece_cross(1)
    finish(7)
    fold(6)
    fold(8)
    finish(4)
    finish(6)
    finish(8)

    def place(ref, k, value):
        for xv in range(4):
            ref[:, pl.ds(256 * xv + 128 * k, 128)] = value[:, 128 * xv : 128 * xv + 128].astype(jnp.bfloat16)

    def wide(value):
        return value.astype(jnp.float32)

    for k in range(2):
        self_home(k).wait_recv()
        place(self_ref.at[0], k, wide(summed[k, yh]) + wide(home_self[k]))

    @pl.when(core == 0)
    def _():
        within_mirror().wait_recv()
        place(cross_ref.at[0, 0], 0, wide(summed[2, yh]) + wide(home_near[0, 0]))
        remote(home_near.at[1, 1], home_near.at[1, 1], home_s.at[2, 0], near_r.at[1, 1], mate).wait_recv()
        remote(home_near.at[2, 1], home_near.at[2, 1], home_s.at[2, 0], near_r.at[2, 1], mate).wait_recv()
        place(cross_ref.at[0, 0], 1, wide(home_near[1, 1]) + wide(home_near[2, 1]))

    mine = jnp.where(yl == 0, 3, 5)

    def gather_home(box, sems, first, out):
        for k in range(2):
            remote(box.at[0, k], box.at[0, k], home_s.at[0, 0], sems.at[0, k], mirror).wait_recv()
        for source in (1, 2):
            remote(box.at[source], box.at[source], home_s.at[0, 0], sems.at[source, 0], mirror).wait_recv()
        for k in range(2):
            place(
                out, k,
                wide(summed[first + k, yh]) + wide(box[0, k]) + wide(box[1, k]) + wide(box[2, k]),
            )

    gather_home(home_far, far_r, mine, cross_ref.at[0, 1])

    @pl.when(core == 1)
    def _():
        gather_home(home_near, near_r, 7, cross_ref.at[0, 0])

    mate_copy(0).wait_send()

    @pl.when(core == 0)
    def _():
        mate_copy(1).wait_send()

    for step in range(8):
        inner_copy(step).wait_send()
        along_copy(step).wait_send()
    for k in range(2):
        cross_copy(k).wait_send()
    for p in range(PIECES):
        for side in range(2):
            hop_copy(p, side).wait_send()
            fold_copy(p, side).wait_send()
        home_op(p, lambda copy: copy.wait_send())


def gram_tiles(own):
    bf16 = jnp.bfloat16
    dma = pltpu.SemaphoreType.DMA
    return pl.pallas_call(
        tiles_kernel,
        out_shape=(
            jax.ShapeDtypeStruct((1, 128, 1024), bf16),
            jax.ShapeDtypeStruct((1, 2, 128, 1024), bf16),
        ),
        in_specs=[pl.BlockSpec(memory_space=pl.ANY)],
        out_specs=(pl.BlockSpec(memory_space=pltpu.VMEM), pl.BlockSpec(memory_space=pltpu.VMEM)),
        scratch_shapes=[
            pltpu.VMEM((14, 512, 1024), bf16),
            pltpu.VMEM((PIECES, 4, 2, 128, 512), bf16),
            pltpu.VMEM((PIECES, 2, 128, 512), bf16),
            pltpu.VMEM((PIECES, 2, 2, 128, 512), bf16),
            pltpu.VMEM((PIECES, 2, 128, 512), bf16),
            pltpu.VMEM((2, 128, 512), bf16),
            pltpu.VMEM((3, 2, 128, 512), bf16),
            pltpu.VMEM((3, 2, 128, 512), bf16),
            dma((2,)), dma((2,)), dma((2,)), dma((8,)), dma((8,)), dma((8,)), dma((8,)), dma((2,)), dma((2,)),
            dma((PIECES, 2)), dma((PIECES, 2)), dma((PIECES, 2)), dma((PIECES, 2)), dma((PIECES, 2)),
            dma((2,)), dma((3, 2)), dma((3, 2)),
        ],
        compiler_params=pltpu.CompilerParams(
            collective_id=0, has_side_effects=True, vmem_limit_bytes=56 * 2**20
        ),
        cost_estimate=pl.CostEstimate(flops=13 * 10**9, bytes_accessed=8 * 2**20, transcendentals=0),
        name="gram_tiles",
    )(own)


def per_device(activations, out_grads, in_factor, out_factor, stored_rows, example_class):
    layer_count = activations.shape[0]
    example_count = activations.shape[1]
    token_count = activations.shape[2]
    model_width = activations.shape[3]
    factor_rank = in_factor.shape[2]
    row_count = stored_rows.shape[0]
    chunked = stored_rows.reshape(4, 2, 128, 2, 1024).transpose(1, 3, 0, 2, 4).reshape(2, 2, 512, 1024)
    self_out, cross_out = gram_tiles(chunked)
    pieces = []
    for layer_index in range(layer_count):
        left_side = jnp.dot(
            activations[layer_index].reshape(-1, model_width),
            in_factor[layer_index],
            preferred_element_type=jnp.float32,
        ).reshape(example_count, token_count, factor_rank)
        right_side = jnp.dot(
            out_grads[layer_index].reshape(-1, model_width),
            out_factor[layer_index],
            preferred_element_type=jnp.float32,
        ).reshape(example_count, token_count, factor_rank)
        outer = jnp.einsum("etp,etq->epq", left_side, right_side, precision=lax.Precision.HIGHEST)
        pieces.append(outer.reshape(example_count, factor_rank * factor_rank))
    fresh = jnp.concatenate(pieces, axis=1)
    one_hot = (example_class[:, None] == jnp.arange(CLASSES, dtype=jnp.int32)[None, :]).astype(
        jnp.float32
    )
    local_sums = jnp.dot(
        one_hot.T, fresh, precision=lax.Precision.HIGHEST, preferred_element_type=jnp.float32
    )
    class_sums = lax.psum(local_sums.astype(jnp.bfloat16), "group")
    score_part = inner_block(class_sums, stored_rows.reshape(row_count, -1))
    score_sums = lax.psum_scatter(
        score_part.astype(jnp.bfloat16), "layer", scatter_dimension=0, tiled=True
    )
    return (self_out, cross_out, score_sums.astype(jnp.bfloat16))


def solution(mesh):
    placed = (
        P("layer", "group", None, None),
        P("layer", "group", None, None),
        P("layer", None, None),
        P("layer", None, None),
        P("group", "layer", None),
        P("group"),
    )
    return jax.shard_map(
        per_device,
        mesh=mesh,
        in_specs=placed,
        out_specs=(P("group", "layer", None), P("group", None, "layer", None), P("layer", "group")),
        check_vma=False,
    )
```

time: 503 us -> 337 us (0.67)
  waiting for transfers between devices: 433 us -> 196 us
  Pallas kernels: 0 us -> 97.1 us
  matrix products: 32.3 us -> 10.7 us
  starting transfers between devices: 8.4 us -> 0.08 us
    reduce_scatter x1 -> x0, waiting for transfers between devices: 109 us -> none  [per_device(): lax.psum_scatter(tiles.astype(jnp.bfloat16), 'layer', scatter_dimension=1...]
    pallas_call x0 -> x1, Pallas kernels: none -> 97.1 us  [gram_tiles(): pl.pallas_call(tiles_kernel, out_shape=(jax.ShapeDtypeStruct((1, 128, 102...]
    unnamed x4 -> x3, waiting for transfers between devices: 63 us -> 0.05 us
    ppermute x2 -> x0, waiting for transfers between devices: 45.7 us -> none  [from_behind(): lax.ppermute(shard, axis, [(i, (i + by) % peers) for i in range(peers)])]
    dot_general x4 -> x1, matrix products: 27.3 us -> 4.24 us  [inner_block(): lax.dot_general(left_rows, right_rows, (((1,), (1,)), ((), ())), preferre...]
    psum x1, waiting for transfers between devices: 214 us -> 196 us  [per_device(): class_sums = lax.psum(local_sums.astype(jnp.bfloat16), 'group')]
    ppermute x2 -> x0, starting transfers between devices: 8.1 us -> none  [from_behind(): lax.ppermute(shard, axis, [(i, (i + by) % peers) for i in range(peers)])]
    reshape x0 -> x1, local copies, waits for them, and re-layouts: none -> 5.63 us  [per_device(): stored_rows.reshape(4, 2, 128, 2, 1024).transpose(1, 3, 0, 2, 4)]
  transfers between devices with their start and end apart: 5 -> 2, of which waited for: 4 -> 1; matrix products, arithmetic and copies ran while one was open for 7% -> 3% of each run, Pallas kernels for 0% -> 29%
where the time goes in v1:
time: 337 us; the launch traced here: 334 us
  waiting for transfers between devices  196 us (58%)
  Pallas kernels  97.1 us (29%)
  between operations  14.8 us (4%)
  local copies, waits for them, and re-layouts  14.7 us (4%)
  matrix products  10.7 us (3%)
    psum x1, waiting for transfers between devices, per_device(): class_sums = lax.psum(local_sums.astype(jnp.bfloat16), 'group')  196 us
    pallas_call x1, Pallas kernels, gram_tiles(): pl.pallas_call(tiles_kernel, out_shape=(jax.ShapeDtypeStruct((1, 128, 102...  97.1 us
    unnamed x15, local copies, waits for them, and re-layouts  8.86 us
  transfers between devices with their start and end apart: 2, of which 1 were waited for; matrix products, arithmetic and copies ran while one was open for 3% of the time, Pallas kernels for 29%

profile of v1, /device:TPU:1, one launch (start us, length us, event | category | flops | bytes accessed | tf_op | source)
XLA Modules:
  0.0 333.5 jit_solution(16836384207792592876)
XLA Ops:
  7.2 0.0 copy-start.2
  7.2 0.0 copy-start.3
  7.2 0.0 all-reduce.4.cloned.1.call-start
  7.2 2.0 fusion.2
  9.2 1.9 fusion.6
  11.1 0.0 copy-done.2
  11.1 0.0 copy-done.3
  11.1 0.0 copy-start.1
  11.1 0.6 fusion
  11.7 0.6 fusion.4
  12.3 0.2 fusion.28
  12.5 0.1 reshape.37
  12.6 0.2 fusion.27
  12.8 0.1 reshape.36
  12.9 0.0 copy-done.1
  12.9 1.1 convolution_convert_fusion
  13.9 0.0 all-reduce.4.cloned.1.call-update
  14.0 0.0 all-reduce.6.cloned.1.call-start
  14.0 0.0 copy-start
  14.0 5.6 %copy.10 = bf16[4,2,128,2,1024]{4,2,0,3,1:T(8,128)(2,1)} copy(bf16[4,2,128,2,1024]{4,3,2,1,0:T(2,128)(2,1)} %bitcast.41) | data formatting | bytes 8388608 | tf_op jit(solution)/shard_map/reshape | solution.py:381
  19.7 0.0 copy-done
  19.7 3.4 %copy.11 = bf16[128,8,2,1024]{3,1,2,0:T(8,128)(2,1)} copy(bf16[128,8,2,1024]{3,2,1,0:T(2,128)(2,1)S(1)} %bitcast.42) | data formatting | bytes 8388608
  23.1 196.1 %all-reduce.4.cloned.1.call-done = bf16[32,2048]{1,0:T(8,128)(2,1)} async-done(((bf16[32,2048]{1,0:T(8,128)(2,1)}), bf16[32,2048]{1,0:T(8,128)(2,1)}) %all-reduce.4.cloned.1.call-update) | async-done | bytes 131088 | tf_op jit(solution)/shard_map/psum | solution.py:404
  219.2 4.2 %convolution_convert_fusion.1 = bf16[32,1024]{1,0:T(8,128)(2,1)} fusion(bf16[32,2048]{1,0:T(8,128)(2,1)} %all-reduce.4.cloned.1.call-done, bf16[1024,2048]{1,0:T(8,128)(2,1)} %bitcast.43), kind=kOutput, calls=%fused_computation.1 | convolution fusion | flops 134250496 | bytes 4390912 | tf_op jit(solution)/shard_map/dot_general | solution.py:17
  223.4 0.0 all-reduce.6.cloned.1.call-update
  223.4 0.0 copy-start.4
  223.4 97.1 %gram_tiles.1 = (bf16[1,128,1024]{2,1,0:T(8,128)(2,1)}, bf16[1,2,128,1024]{3,2,1,0:T(8,128)(2,1)}) custom-call(bf16[2,2,512,1024]{3,2,1,0:T(8,128)(2,1)} %bitcast.44), custom_call_target="tpu_custom_call" | custom-call | flops 12999999488 | bytes 8388608 | tf_op jit(solution)/shard_map/gram_tiles/pallas_call | solution.py:345
  320.5 0.6 dynamic-slice
  321.8 0.0 all-reduce.6.cloned.1.call-done
  321.8 1.3 constant_dynamic-slice_fusion
  323.1 1.7 copy.16
  324.8 1.9 copy.17
  (1 shorter events, 0.0 us)
Async XLA Ops:
  7.2 4.0 %copy-start.2 = (bf16[2,2,64,4096]{3,2,1,0:T(8,128)(2,1)S(1)}, bf16[2,2,64,4096]{3,2,1,0:T(8,128)(2,1)}, u32[]{:S(2)}) copy-start(bf16[2,2,64,4096]{3,2,1,0:T(8,128)(2,1)} %param.7) | copy-start | bytes 6291460
  7.2 4.0 %copy-start.3 = (bf16[2,4096,32]{1,2,0:T(8,128)(2,1)S(1)}, bf16[2,4096,32]{1,2,0:T(8,128)(2,1)}, u32[]{:S(2)}) copy-start(bf16[2,4096,32]{1,2,0:T(8,128)(2,1)} %param.9) | copy-start | bytes 1572868
  7.2 212.0 %all-reduce.4.cloned.1.call-start = ((), (), s32[]{:S(2)}) async-start(), calls=%async_computation | async-start | bytes 262144 | tf_op jit(solution)/shard_map/psum | solution.py:404
  11.1 1.7 copy-start.1
  14.0 307.8 %all-reduce.6.cloned.1.call-start = ((), (), s32[]{:S(2)}) async-start(), calls=%async_computation.1 | async-start | bytes 131072
  14.0 5.6 %copy-start = (bf16[1024,2,1024]{2,1,0:T(2,128)(2,1)S(1)}, bf16[1024,2,1024]{2,1,0:T(2,128)(2,1)}, u32[]{:S(2)}) copy-start(bf16[1024,2,1024]{2,1,0:T(2,128)(2,1)} %param.10) | copy-start | bytes 12582916
  223.4 97.1 %copy-start.4 = (u32[256]{0:T(256)S(1)}, u32[256]{0:T(256)}, u32[]{:S(2)}) copy-start(u32[256]{0:T(256)} %constant.8) | copy-start | bytes 3076
Sparse Core Ops, SparseCore 0:
  14.1 205.0 all-reduce.3
  223.5 86.1 all-reduce.5

commit v2 on v1

--- a/solution.py
+++ b/solution.py
@@ -7,7 +7,7 @@
 from jax.experimental.pallas import tpu as pltpu
 from jax.sharding import PartitionSpec as P
 
-CLASSES = 32
+RANK = 32
 MESH = pl.DeviceIdType.MESH
 OWN, MATE, INNER, ALONG, CROSS = 0, 4, 8, 10, 12
 PIECES = 9
@@ -20,8 +20,11 @@
 
 
 def tiles_kernel(
-    own_hbm, self_ref, cross_ref,
+    own_hbm, acts_hbm, grads_hbm, in_hbm, out_hbm, class_ref, self_ref, cross_ref, score_ref,
     chunks, parts, hop, near_in, summed, home_self, home_near, home_far,
+    acts, grads, in_rows, out_rows, note, notes, class_rows,
+    score_parts, score_hop, score_near, score_sum, score_home,
+    load_sem, ring_s, ring_r, share_s, share_r, sc_hop_s, sc_hop_r, sc_fold_s, sc_fold_r, sc_home_s, sc_home_r,
     own_sem, mate_s, mate_r, inner_s, inner_r, along_s, along_r, cross_s, cross_r,
     hop_s, hop_r, fold_s, fold_r, home_s, self_r, near_r, far_r,
 ):
@@ -42,7 +45,7 @@
     greeted = [right, left, mirror]
     for step in (1, -1, 2, -2):
         greeted += [at(x, yh, group + step), at(x, other, group + step)]
-    greeted += [at(x, yh, group + 4), at(x, yh, group - 4)]
+    greeted += [at(x, yh, group + 4 * step) for step in range(1, 8)]
     barrier = pltpu.get_barrier_semaphore()
     for who in greeted:
         pl.semaphore_signal(barrier, inc=1, device_id=who, device_id_type=MESH)
@@ -50,7 +53,13 @@
         pltpu.make_async_copy(own_hbm.at[k], chunks.at[pl.ds(OWN + 2 * k, 2)], own_sem.at[k])
         for k in range(2)
     ]
-    for copy in own_copies:
+    loads = [
+        pltpu.make_async_copy(src, dst, load_sem.at[k])
+        for k, (src, dst) in enumerate(
+            [(acts_hbm, acts), (grads_hbm, grads), (in_hbm, in_rows), (out_hbm, out_rows)]
+        )
+    ]
+    for copy in own_copies + loads:
         copy.start()
     pl.semaphore_wait(barrier, len(greeted))
 
@@ -228,6 +237,114 @@
         cross_copy(k).wait_recv()
         half_piece(7 + k, CROSS + k, core == 0)
 
+    def ring_copy(step):
+        return remote(
+            notes.at[0, 0], notes.at[0, step], ring_s.at[step - 1], ring_r.at[step - 1],
+            at(x, yh, group + 4 * step),
+        )
+
+    def share_copy(k):
+        source, place, who = [(0, 2, across), (0, 1, mate), (2, 3, mate)][k]
+        return remote(notes.at[source], notes.at[place], share_s.at[k], share_r.at[k], who)
+
+    def exact_spread(value, spread):
+        total = None
+        for _ in range(3):
+            part = value.astype(jnp.bfloat16)
+            value = value - part.astype(jnp.float32)
+            term = jnp.dot(part, spread, preferred_element_type=jnp.float32)
+            total = term if total is None else total + term
+        return total
+
+    def project():
+        for copy in loads:
+            copy.wait()
+        feature = lax.broadcasted_iota(jnp.int32, (RANK, RANK * RANK), 1)
+        factor = lax.broadcasted_iota(jnp.int32, (RANK, RANK * RANK), 0)
+        to_p = (feature // RANK == factor).astype(jnp.float32).astype(jnp.bfloat16)
+        to_q = (feature % RANK == factor).astype(jnp.float32).astype(jnp.bfloat16)
+        for k in range(2):
+            left_side = exact_spread(inner_block(acts[k], in_rows[k]), to_p)
+            right_side = exact_spread(inner_block(grads[k], out_rows[k]), to_q)
+            outer = left_side * right_side
+            for e in range(2):
+                fresh = jnp.sum(outer[64 * e : 64 * e + 64], axis=0, keepdims=True)
+                for c in range(4):
+                    row = 8 * e + 4 * k + c
+                    note[row : row + 1, 0:256] = fresh[:, 256 * c : 256 * c + 256]
+        for e in range(2):
+            note[8 * e : 8 * e + 8, 256:384] = jnp.full((8, 128), class_ref[e], jnp.int32).astype(jnp.float32)
+        notes[0, 0] = note[...].astype(jnp.bfloat16)
+        for step in range(1, 8):
+            ring_copy(step).start()
+
+    def share_first():
+        for step in range(1, 8):
+            ring_copy(step).wait_recv()
+        share_copy(0).start()
+        share_copy(1).start()
+
+    def share_second():
+        share_copy(0).wait_recv()
+        share_copy(2).start()
+
+    def score_hop_copy(side):
+        return remote(
+            score_parts.at[lax.rem(x + 2, 4), side], score_hop.at[side], sc_hop_s.at[side], sc_hop_r.at[side],
+            right if side == 0 else left,
+        )
+
+    def score_fold_copy(side):
+        to = lax.rem(x + 1, 4) if side == 0 else lax.rem(x + 3, 4)
+        return remote(
+            score_parts.at[to], score_near.at[side], sc_fold_s.at[side], sc_fold_r.at[side],
+            right if side == 0 else left,
+        )
+
+    def score_home_copy():
+        return remote(score_sum, score_home, sc_home_s, sc_home_r, mirror)
+
+    def score_compute():
+        share_copy(1).wait_recv()
+        share_copy(2).wait_recv()
+        rows = notes[...].reshape(512, 384)
+        fresh = rows[:, 0:256]
+        classes = rows[:, 256:384].astype(jnp.float32).T[0:64]
+        spot = lax.broadcasted_iota(jnp.int32, (64, 512), 0)
+        wanted = jnp.where(spot % 16 < 8, spot // 16 * 8 + spot % 16, -1).astype(jnp.float32)
+        column = lax.broadcasted_iota(jnp.int32, (64, 512), 1) % 8
+        for c in range(8):
+            picked = jnp.where((classes == wanted) & (column == c), 1.0, 0.0).astype(jnp.bfloat16)
+            class_rows[:, 256 * c : 256 * c + 256] = jnp.dot(
+                picked, fresh, preferred_element_type=jnp.float32
+            ).astype(jnp.bfloat16)
+        for k in range(2):
+            part = inner_block(class_rows[:, 0:1024], chunks[OWN + 2 * k]) + inner_block(
+                class_rows[:, 1024:2048], chunks[OWN + 2 * k + 1]
+            )
+            score_parts[:, k] = part.astype(jnp.bfloat16).reshape(4, 16, 512)
+        for side in range(2):
+            score_hop_copy(side).start()
+
+    def score_fold():
+        for side in range(2):
+            to = lax.rem(x + 1, 4) if side == 0 else lax.rem(x + 3, 4)
+            score_hop_copy(side).wait_recv()
+            score_parts[to, side] = (
+                score_parts[to, side].astype(jnp.float32) + score_hop[side].astype(jnp.float32)
+            ).astype(jnp.bfloat16)
+            score_fold_copy(side).start()
+
+    def score_finish():
+        for side in range(2):
+            score_fold_copy(side).wait_recv()
+        score_sum[...] = (
+            score_parts[x].astype(jnp.float32)
+            + score_near[0].astype(jnp.float32)
+            + score_near[1].astype(jnp.float32)
+        ).astype(jnp.bfloat16)
+        score_home_copy().start()
+
     for copy in own_copies:
         copy.wait()
     for k in range(2):
@@ -248,9 +365,11 @@
     )
     fold(1)
     pass_on(1)
+    project()
     finish(0)
     pass_on(2)
     fold(2)
+    share_first()
     pass_on(3)
     cross_inner(0)
     piece_inner(0)
@@ -258,19 +377,23 @@
     take_along(0)
     cross_along(0)
     piece_along(0)
+    share_second()
     pass_on(4)
     fold(3)
     piece_cross(0)
+    score_compute()
     finish(2)
     pass_on(5)
     fold(5)
     fold(7)
+    score_fold()
     pass_on(6)
     finish(3)
     pass_on(7)
     cross_inner(1)
     piece_inner(1)
     finish(5)
+    score_finish()
     take_along(1)
     cross_along(1)
     piece_along(1)
@@ -321,6 +444,19 @@
     def _():
         gather_home(home_near, near_r, 7, cross_ref.at[0, 0])
 
+    score_home_copy().wait_recv()
+    for k in range(2):
+        scores = wide(score_sum[k]) + wide(score_home[k])
+        place(score_ref, k, jnp.where(yh == 0, scores[0:4], scores[4:8]))
+
+    score_home_copy().wait_send()
+    for side in range(2):
+        score_hop_copy(side).wait_send()
+        score_fold_copy(side).wait_send()
+    for step in range(1, 8):
+        ring_copy(step).wait_send()
+    for k in range(3):
+        share_copy(k).wait_send()
     mate_copy(0).wait_send()
 
     @pl.when(core == 0)
@@ -339,7 +475,7 @@
         home_op(p, lambda copy: copy.wait_send())
 
 
-def gram_tiles(own):
+def gram_tiles(own, acts, grads, in_rows, out_rows, classes):
     bf16 = jnp.bfloat16
     dma = pltpu.SemaphoreType.DMA
     return pl.pallas_call(
@@ -347,9 +483,10 @@
         out_shape=(
             jax.ShapeDtypeStruct((1, 128, 1024), bf16),
             jax.ShapeDtypeStruct((1, 2, 128, 1024), bf16),
+            jax.ShapeDtypeStruct((4, 1024), bf16),
         ),
-        in_specs=[pl.BlockSpec(memory_space=pl.ANY)],
-        out_specs=(pl.BlockSpec(memory_space=pltpu.VMEM), pl.BlockSpec(memory_space=pltpu.VMEM)),
+        in_specs=[pl.BlockSpec(memory_space=pl.ANY)] * 5 + [pl.BlockSpec(memory_space=pltpu.SMEM)],
+        out_specs=(pl.BlockSpec(memory_space=pltpu.VMEM),) * 3,
         scratch_shapes=[
             pltpu.VMEM((14, 512, 1024), bf16),
             pltpu.VMEM((PIECES, 4, 2, 128, 512), bf16),
@@ -359,6 +496,20 @@
             pltpu.VMEM((2, 128, 512), bf16),
             pltpu.VMEM((3, 2, 128, 512), bf16),
             pltpu.VMEM((3, 2, 128, 512), bf16),
+            pltpu.VMEM((2, 128, 4096), bf16),
+            pltpu.VMEM((2, 128, 4096), bf16),
+            pltpu.VMEM((2, RANK, 4096), bf16),
+            pltpu.VMEM((2, RANK, 4096), bf16),
+            pltpu.VMEM((16, 384), jnp.float32),
+            pltpu.VMEM((4, 8, 16, 384), bf16),
+            pltpu.VMEM((64, 2048), bf16),
+            pltpu.VMEM((4, 2, 16, 512), bf16),
+            pltpu.VMEM((2, 16, 512), bf16),
+            pltpu.VMEM((2, 2, 16, 512), bf16),
+            pltpu.VMEM((2, 16, 512), bf16),
+            pltpu.VMEM((2, 16, 512), bf16),
+            dma((4,)), dma((7,)), dma((7,)), dma((3,)), dma((3,)),
+            dma((2,)), dma((2,)), dma((2,)), dma((2,)), dma, dma,
             dma((2,)), dma((2,)), dma((2,)), dma((8,)), dma((8,)), dma((8,)), dma((8,)), dma((2,)), dma((2,)),
             dma((PIECES, 2)), dma((PIECES, 2)), dma((PIECES, 2)), dma((PIECES, 2)), dma((PIECES, 2)),
             dma((2,)), dma((3, 2)), dma((3, 2)),
@@ -368,45 +519,21 @@
         ),
         cost_estimate=pl.CostEstimate(flops=13 * 10**9, bytes_accessed=8 * 2**20, transcendentals=0),
         name="gram_tiles",
-    )(own)
+    )(own, acts, grads, in_rows, out_rows, classes)
 
 
 def per_device(activations, out_grads, in_factor, out_factor, stored_rows, example_class):
     layer_count = activations.shape[0]
-    example_count = activations.shape[1]
-    token_count = activations.shape[2]
     model_width = activations.shape[3]
-    factor_rank = in_factor.shape[2]
-    row_count = stored_rows.shape[0]
     chunked = stored_rows.reshape(4, 2, 128, 2, 1024).transpose(1, 3, 0, 2, 4).reshape(2, 2, 512, 1024)
-    self_out, cross_out = gram_tiles(chunked)
-    pieces = []
-    for layer_index in range(layer_count):
-        left_side = jnp.dot(
-            activations[layer_index].reshape(-1, model_width),
-            in_factor[layer_index],
-            preferred_element_type=jnp.float32,
-        ).reshape(example_count, token_count, factor_rank)
-        right_side = jnp.dot(
-            out_grads[layer_index].reshape(-1, model_width),
-            out_factor[layer_index],
-            preferred_element_type=jnp.float32,
-        ).reshape(example_count, token_count, factor_rank)
-        outer = jnp.einsum("etp,etq->epq", left_side, right_side, precision=lax.Precision.HIGHEST)
-        pieces.append(outer.reshape(example_count, factor_rank * factor_rank))
-    fresh = jnp.concatenate(pieces, axis=1)
-    one_hot = (example_class[:, None] == jnp.arange(CLASSES, dtype=jnp.int32)[None, :]).astype(
-        jnp.float32
+    return gram_tiles(
+        chunked,
+        activations.reshape(layer_count, -1, model_width),
+        out_grads.reshape(layer_count, -1, model_width),
+        in_factor.transpose(0, 2, 1),
+        out_factor.transpose(0, 2, 1),
+        example_class,
     )
-    local_sums = jnp.dot(
-        one_hot.T, fresh, precision=lax.Precision.HIGHEST, preferred_element_type=jnp.float32
-    )
-    class_sums = lax.psum(local_sums.astype(jnp.bfloat16), "group")
-    score_part = inner_block(class_sums, stored_rows.reshape(row_count, -1))
-    score_sums = lax.psum_scatter(
-        score_part.astype(jnp.bfloat16), "layer", scatter_dimension=0, tiled=True
-    )
-    return (self_out, cross_out, score_sums.astype(jnp.bfloat16))
 
 
 def solution(mesh):

time: 337 us -> 131 us (0.39); the launches traced: 334 us -> 131 us
  waiting for transfers between devices: 196 us -> 0 us
  Pallas kernels: 97.1 us -> 120 us
  between operations: 14.8 us -> 0.64 us
  matrix products: 10.7 us -> 0 us
  local copies, waits for them, and re-layouts: 14.7 us -> 10.3 us
    psum x1 -> x0, waiting for transfers between devices: 196 us -> none  [per_device(): class_sums = lax.psum(local_sums.astype(jnp.bfloat16), 'group')]
    pallas_call x1, Pallas kernels: 97.1 us -> 120 us  [gram_tiles(): pl.pallas_call(tiles_kernel, out_shape=(jax.ShapeDtypeStruct((1, 128, 102...]
    dot_general x8 -> x0, matrix products: 10.7 us -> none  [the longest x1 4.24 us: inner_block(): lax.dot_general(left_rows, right_rows, (((1,), (1,)), ((), ())), preferre...]
    unnamed x15 -> x3, local copies, waits for them, and re-layouts: 8.86 us -> 4.84 us
  transfers between devices with their start and end apart: 2 -> 0, of which waited for: 1 -> 0; matrix products, arithmetic and copies ran while one was open for 3% -> 0% of each run, Pallas kernels for 29% -> 0%
where the time goes in v2:
time: 131 us
  Pallas kernels  120 us (92%)
  local copies, waits for them, and re-layouts  10.3 us (8%)
    pallas_call x1, Pallas kernels, gram_tiles(): pl.pallas_call(tiles_kernel, out_shape=(jax.ShapeDtypeStruct((1, 128, 102...  120 us
    reshape x1, local copies, waits for them, and re-layouts, per_device(): stored_rows.reshape(4, 2, 128, 2, 1024).transpose(1, 3, 0, 2, 4)  5.47 us
    unnamed x3, local copies, waits for them, and re-layouts  4.84 us

profile of v2, /device:TPU:1, one launch (start us, length us, event | category | flops | bytes accessed | tf_op | source)
XLA Modules:
  0.0 131.2 jit_solution(1574271170913881031)
XLA Ops:
  0.6 5.5 %copy.9 = bf16[4,2,128,2,1024]{4,2,0,3,1:T(8,128)(2,1)} copy(bf16[4,2,128,2,1024]{4,3,2,1,0:T(2,128)(2,1)} %bitcast.8) | data formatting | bytes 8388608 | tf_op jit(solution)/shard_map/reshape | solution.py:528
  6.1 120.2 %gram_tiles.1 = (bf16[1,128,1024]{2,1,0:T(8,128)(2,1)}, bf16[1,2,128,1024]{3,2,1,0:T(8,128)(2,1)}, bf16[4,1024]{1,0:T(4,128)(2,1)}) custom-call(bf16[2,2,512,1024]{3,2,1,0:T(8,128)(2,1)} %bitcast.9, bf16[2,128,4096]{2,1,0:T(8,128)(2,1)} %bitcast.10, bf16[2,128,4096]{2,1,0:T(8,128)(2,1)} %bitcast.11, bf16[2,32,4096]{2,1,0:T(8,128)(2,1)} %bitcast.12, ...), custom_call_target="tpu_custom_call" | custom-call | flops 12999999488 | bytes 8388608 | tf_op jit(solution)/shard_map/gram_tiles/pallas_call | solution.py:481
  126.3 1.7 %copy.13 = bf16[1,128,1024]{2,1,0:T(8,128)(2,1)} copy(bf16[1,128,1024]{2,1,0:T(8,128)(2,1)} %get-tuple-element.6) | data formatting | bytes 524288
  128.0 1.9 %copy.14 = bf16[1,2,128,1024]{3,2,1,0:T(8,128)(2,1)} copy(bf16[1,2,128,1024]{3,2,1,0:T(8,128)(2,1)} %get-tuple-element.7) | data formatting | bytes 1048576
  129.9 1.3 copy.15

commit v3 on v2

--- a/solution.py
+++ b/solution.py
@@ -20,11 +20,11 @@
 
 
 def tiles_kernel(
-    own_hbm, acts_hbm, grads_hbm, in_hbm, out_hbm, class_ref, self_ref, cross_ref, score_ref,
+    stored_hbm, acts_hbm, grads_hbm, in_hbm, out_hbm, class_ref, self_ref, cross_ref, score_ref,
     chunks, parts, hop, near_in, summed, home_self, home_near, home_far,
     acts, grads, in_rows, out_rows, note, notes, class_rows,
     score_parts, score_hop, score_near, score_sum, score_home,
-    load_sem, ring_s, ring_r, share_s, share_r, sc_hop_s, sc_hop_r, sc_fold_s, sc_fold_r, sc_home_s, sc_home_r,
+    raw, turn_out, turn_in, turn_s, turn_r, load_sem, ring_s, ring_r, share_s, share_r, sc_hop_s, sc_hop_r, sc_fold_s, sc_fold_r, sc_home_s, sc_home_r,
     own_sem, mate_s, mate_r, inner_s, inner_r, along_s, along_r, cross_s, cross_r,
     hop_s, hop_r, fold_s, fold_r, home_s, self_r, near_r, far_r,
 ):
@@ -46,12 +46,13 @@
     for step in (1, -1, 2, -2):
         greeted += [at(x, yh, group + step), at(x, other, group + step)]
     greeted += [at(x, yh, group + 4 * step) for step in range(1, 8)]
+    greeted += [at(x + step, other, group) for step in range(1, 4)]
     barrier = pltpu.get_barrier_semaphore()
     for who in greeted:
         pl.semaphore_signal(barrier, inc=1, device_id=who, device_id_type=MESH)
     own_copies = [
-        pltpu.make_async_copy(own_hbm.at[k], chunks.at[pl.ds(OWN + 2 * k, 2)], own_sem.at[k])
-        for k in range(2)
+        pltpu.make_async_copy(stored_hbm.at[rows], raw.at[rows], own_sem.at[step])
+        for step, rows in enumerate([pl.ds(256 * (step % 4) + 128 * (step // 4), 128) for step in range(8)])
     ]
     loads = [
         pltpu.make_async_copy(src, dst, load_sem.at[k])
@@ -61,6 +62,22 @@
     ]
     for copy in own_copies + loads:
         copy.start()
+    pair = lax.broadcasted_iota(jnp.int32, (128, 256), 1)
+    wanted_row = lax.broadcasted_iota(jnp.int32, (128, 256), 0) * 2
+    pick = [(pair == wanted_row + f).astype(jnp.float32).astype(jnp.bfloat16) for f in range(2)]
+    for copy in own_copies:
+        copy.wait()
+
+    def take_apart(step, carry):
+        k, xv = step // 4, step % 4
+        rows = raw[pl.ds(pl.multiple_of(256 * xv + 128 * k, 128), 128)].reshape(256, 1024)
+        for f in range(2):
+            chunks[OWN + 2 * k + f, pl.ds(pl.multiple_of(128 * xv, 128), 128), :] = jnp.dot(
+                pick[f], rows, preferred_element_type=jnp.float32
+            ).astype(jnp.bfloat16)
+        return carry
+
+    lax.fori_loop(0, 8, take_apart, 0)
     pl.semaphore_wait(barrier, len(greeted))
 
     def remote(src, dst, send, recv, who):
@@ -73,7 +90,7 @@
 
     def inner_copy(step):
         k, rows = rows_of(step)
-        return remote(own_hbm.at[k, yl, rows], chunks.at[INNER + k, rows], inner_s.at[step], inner_r.at[step], across)
+        return remote(chunks.at[OWN + 2 * k + yl, rows], chunks.at[INNER + k, rows], inner_s.at[step], inner_r.at[step], across)
 
     def along_copy(step):
         k, rows = rows_of(step)
@@ -82,7 +99,7 @@
         )
 
     def mate_copy(k):
-        return remote(own_hbm.at[k], chunks.at[pl.ds(MATE + 2 * k, 2)], mate_s.at[k], mate_r.at[k], mate)
+        return remote(chunks.at[pl.ds(OWN + 2 * k, 2)], chunks.at[pl.ds(MATE + 2 * k, 2)], mate_s.at[k], mate_r.at[k], mate)
 
     passes_inner = yl == core
     passed = jnp.where(passes_inner, INNER, ALONG)
@@ -90,20 +107,27 @@
     def cross_copy(k):
         return remote(chunks.at[passed + k], chunks.at[CROSS + k], cross_s.at[k], cross_r.at[k], mate)
 
+    def share(p, ref, h):
+        if p == 0:
+            return ref.at[h, :, pl.ds(0, 384)]
+        if p == 1:
+            return ref.at[0, :, pl.ds(256 * h, 256)]
+        return ref.at[h]
+
     def hop_copy(p, side):
         return remote(
-            parts.at[p, lax.rem(x + 2, 4), side], hop.at[p, side], hop_s.at[p, side], hop_r.at[p, side],
-            right if side == 0 else left,
-        )
-
-    def fold_copy(p, side):
+            share(p, parts.at[p, lax.rem(x + 2, 4)], side), share(p, hop.at[p], side),
+            hop_s.at[p, side], hop_r.at[p, side], right if side == 0 else left,
+        )
+
+    def fold_copy(p, side, h):
         to = lax.rem(x + 1, 4) if side == 0 else lax.rem(x + 3, 4)
         return remote(
-            parts.at[p, to], near_in.at[p, side], fold_s.at[p, side], fold_r.at[p, side],
-            right if side == 0 else left,
-        )
-
-    for step in range(8):
+            share(p, parts.at[p, to], h), share(p, near_in.at[p, side], h),
+            fold_s.at[p, side, h], fold_r.at[p, side, h], right if side == 0 else left,
+        )
+
+    for step in range(4):
         inner_copy(step).start()
     mate_copy(0).start()
 
@@ -111,22 +135,44 @@
     def _():
         mate_copy(1).start()
 
+    def send_shares(p):
+        for side in range(2):
+            hop_copy(p, side).start()
+        for side in range(2):
+            fold_copy(p, side, 1 - side).start()
+
+    def product(lefts, rights, cols):
+        total = None
+        for a, b in zip(lefts, rights):
+            term = inner_block(chunks[a], chunks[b, cols, :])
+            total = term if total is None else total + term
+        return total.astype(jnp.bfloat16).reshape(4, 128, 256)
+
+    def diagonal():
+        for i in range(2):
+            slots = [OWN + 2 * i, OWN + 2 * i + 1]
+            for n in range(2):
+                total = product(slots, slots, pl.ds(256 * n, 256))
+                for xu in range(4):
+                    for xv in (2 * n, 2 * n + 1):
+                        d = (xv - xu) % 4
+                        if d < 3:
+                            parts[0, xu, i, :, 128 * d : 128 * d + 128] = total[
+                                xu, :, 128 * (xv - 2 * n) : 128 * (xv - 2 * n) + 128
+                            ]
+        send_shares(0)
+
     def compute(p, left_slots, right_slots):
-        for i in range(2):
+        for i in range(1 if p == 1 else 2):
             lefts, rights = left_slots(i), right_slots(i)
 
             def columns(n, carry):
                 cols = pl.ds(pl.multiple_of(n * 256, 256), 256)
-                total = None
-                for a, b in zip(lefts, rights):
-                    term = inner_block(chunks[a], chunks[b, cols, :])
-                    total = term if total is None else total + term
-                parts[p, :, i, :, cols] = total.astype(jnp.bfloat16).reshape(4, 128, 256)
+                parts[p, :, i, :, cols] = product(lefts, rights, cols)
                 return carry
 
             lax.fori_loop(0, 2, columns, 0)
-        for side in range(2):
-            hop_copy(p, side).start()
+        send_shares(p)
 
     half = 1 - yl
 
@@ -143,55 +189,77 @@
         for side in range(2):
             to = lax.rem(x + 1, 4) if side == 0 else lax.rem(x + 3, 4)
             hop_copy(p, side).wait_recv()
-            parts[p, to, side] = (
-                parts[p, to, side].astype(jnp.float32) + hop[p, side].astype(jnp.float32)
-            ).astype(jnp.bfloat16)
-            fold_copy(p, side).start()
-
-    def total_of(p):
-        for side in range(2):
-            fold_copy(p, side).wait_recv()
-        summed[p] = (
-            parts[p, x].astype(jnp.float32)
-            + near_in[p, 0].astype(jnp.float32)
-            + near_in[p, 1].astype(jnp.float32)
+            mine, come = share(p, parts.at[p, to], side), share(p, hop.at[p], side)
+            mine[...] = (mine[...].astype(jnp.float32) + come[...].astype(jnp.float32)).astype(jnp.bfloat16)
+            fold_copy(p, side, side).start()
+
+    def total_of(p, h):
+        for side in range(2):
+            fold_copy(p, side, h).wait_recv()
+        share(p, summed.at[p], h)[...] = (
+            share(p, parts.at[p, x], h)[...].astype(jnp.float32)
+            + share(p, near_in.at[p, 0], h)[...].astype(jnp.float32)
+            + share(p, near_in.at[p, 1], h)[...].astype(jnp.float32)
         ).astype(jnp.bfloat16)
 
-    def self_home(k):
-        return remote(summed.at[k, other], home_self.at[k], home_s.at[k, 0], self_r.at[k], mirror)
-
-    def within_mirror():
-        return remote(summed.at[2, other], home_near.at[0, 0], home_s.at[2, 0], near_r.at[0, 0], mirror)
-
-    def within_mate():
-        return remote(summed.at[2, yh], home_near.at[1, 1], home_s.at[2, 0], near_r.at[1, 1], mate)
-
-    def within_mate_mirror():
-        return remote(
-            summed.at[2, other], home_near.at[2, 1], home_s.at[2, 1], near_r.at[2, 1],
+    def diagonal_home(h):
+        return remote(share(0, summed.at[0], h), home_self.at[0, :, pl.ds(0, 384)], home_s.at[0, h], self_r.at[0], mirror)
+
+    def beside_home():
+        return remote(summed.at[1, 0], home_self.at[1], home_s.at[1, 0], self_r.at[1], mirror)
+
+    def turn_copy(xv):
+        return remote(turn_out.at[xv], turn_in.at[x], turn_s.at[xv], turn_r.at[x], at(xv, 1, group))
+
+    def next_copy():
+        return remote(turn_out.at[4], turn_in.at[4], turn_s.at[4], turn_r.at[4], right)
+
+    def within_mirror(h):
+        return remote(summed.at[2, h], home_near.at[0, 0], home_s.at[2, h], near_r.at[0, 0], mirror)
+
+    def within_mate(h):
+        return remote(summed.at[2, h], home_near.at[1, 1], home_s.at[2, h], near_r.at[1, 1], mate)
+
+    def within_mate_mirror(h):
+        return remote(
+            summed.at[2, h], home_near.at[2, 1], home_s.at[2, h], near_r.at[2, 1],
             at(x, other, group + 1 - 2 * core),
         )
 
-    def col_home(p, k, box, sems):
-        return remote(summed.at[p, other], box.at[0, k], home_s.at[p, 0], sems.at[0, k], mirror)
-
-    def row_home(p, k, box, sems, back):
+    def col_home(p, k, h, box, sems):
+        return remote(summed.at[p, h], box.at[0, k], home_s.at[p, h], sems.at[0, k], mirror)
+
+    def row_home(p, k, h, box, sems, back):
         place = jnp.where(yh == k, 1, 2)
-        return remote(summed.at[p], box.at[place], home_s.at[p, 0], sems.at[place, 0], at(x, k, group - back))
-
-    def home_op(p, op):
-        if p < 2:
-            op(self_home(p))
+        return remote(
+            summed.at[p, h], box.at[place, h], home_s.at[p, h], sems.at[place, h], at(x, k, group - back)
+        )
+
+    def home_op(p, h, op):
+        if p == 0:
+
+            @pl.when(other == h)
+            def _():
+                op(diagonal_home(h))
+        elif p == 1:
+            if h == 1:
+
+                @pl.when(yh == 1)
+                def _():
+                    op(beside_home())
         elif p == 2:
 
-            @pl.when(core == 0)
+            @pl.when((core == 0) & (other == h))
             def _():
-                op(within_mirror())
-
-            @pl.when(core == 1)
+                op(within_mirror(h))
+
+            @pl.when((core == 1) & (yh == h))
             def _():
-                op(within_mate())
-                op(within_mate_mirror())
+                op(within_mate(h))
+
+            @pl.when((core == 1) & (other == h))
+            def _():
+                op(within_mate_mirror(h))
         else:
             k = (p - 3) % 2
             is_row = {0: yl == 1, 1: yl == 0, 2: core == 0}[(p - 3) // 2]
@@ -199,19 +267,22 @@
 
             @pl.when(is_row)
             def _():
-                op(row_home(p, k, box, sems, back))
-
-            @pl.when(jnp.logical_not(is_row))
+                op(row_home(p, k, h, box, sems, back))
+
+            @pl.when(jnp.logical_not(is_row) & (other == h))
             def _():
-                op(col_home(p, k, box, sems))
+                op(col_home(p, k, h, box, sems))
 
     def finish(p):
-        total_of(p)
-        home_op(p, lambda copy: copy.start())
+        for h in range(2):
+            total_of(p, h)
+            home_op(p, h, lambda copy: copy.start())
 
     def pass_on(step):
         inner_copy(step).wait_recv()
         along_copy(step).start()
+        if step < 4:
+            inner_copy(step + 4).start()
 
     def take_along(k):
         for step in range(4 * k, 4 * k + 4):
@@ -237,15 +308,17 @@
         cross_copy(k).wait_recv()
         half_piece(7 + k, CROSS + k, core == 0)
 
+    def over_copy():
+        return remote(notes.at[0, 0, 0], notes.at[0, 0, 1], share_s.at[0], share_r.at[0], across)
+
     def ring_copy(step):
         return remote(
             notes.at[0, 0], notes.at[0, step], ring_s.at[step - 1], ring_r.at[step - 1],
             at(x, yh, group + 4 * step),
         )
 
-    def share_copy(k):
-        source, place, who = [(0, 2, across), (0, 1, mate), (2, 3, mate)][k]
-        return remote(notes.at[source], notes.at[place], share_s.at[k], share_r.at[k], who)
+    def note_mate_copy():
+        return remote(notes.at[0], notes.at[1], share_s.at[1], share_r.at[1], mate)
 
     def exact_spread(value, spread):
         total = None
@@ -274,19 +347,18 @@
                     note[row : row + 1, 0:256] = fresh[:, 256 * c : 256 * c + 256]
         for e in range(2):
             note[8 * e : 8 * e + 8, 256:384] = jnp.full((8, 128), class_ref[e], jnp.int32).astype(jnp.float32)
-        notes[0, 0] = note[...].astype(jnp.bfloat16)
+        notes[0, 0, 0] = note[...].astype(jnp.bfloat16)
+        over_copy().start()
+
+    def share_first():
+        over_copy().wait_recv()
         for step in range(1, 8):
             ring_copy(step).start()
 
-    def share_first():
+    def share_second():
         for step in range(1, 8):
             ring_copy(step).wait_recv()
-        share_copy(0).start()
-        share_copy(1).start()
-
-    def share_second():
-        share_copy(0).wait_recv()
-        share_copy(2).start()
+        note_mate_copy().start()
 
     def score_hop_copy(side):
         return remote(
@@ -305,8 +377,7 @@
         return remote(score_sum, score_home, sc_home_s, sc_home_r, mirror)
 
     def score_compute():
-        share_copy(1).wait_recv()
-        share_copy(2).wait_recv()
+        note_mate_copy().wait_recv()
         rows = notes[...].reshape(512, 384)
         fresh = rows[:, 0:256]
         classes = rows[:, 256:384].astype(jnp.float32).T[0:64]
@@ -345,10 +416,46 @@
         ).astype(jnp.bfloat16)
         score_home_copy().start()
 
-    for copy in own_copies:
-        copy.wait()
-    for k in range(2):
-        compute(k, lambda i: [OWN + 2 * i, OWN + 2 * i + 1], lambda i: [OWN + 2 * k, OWN + 2 * k + 1])
+    def place(ref, k, value):
+        for xv in range(4):
+            ref[:, pl.ds(256 * xv + 128 * k, 128)] = value[:, 128 * xv : 128 * xv + 128].astype(jnp.bfloat16)
+
+    def wide(value):
+        return value.astype(jnp.float32)
+
+    def column(xv, k):
+        return pl.ds(pl.multiple_of(256 * xv + 128 * k, 128), 128)
+
+    def turn():
+        remote(home_self.at[0, :, pl.ds(0, 384)], home_self.at[0, :, pl.ds(0, 384)], home_s.at[0, 0], self_r.at[0], mirror).wait_recv()
+        diag = (wide(summed[0, yh, :, 0:384]) + wide(home_self[0, :, 0:384])).astype(jnp.bfloat16)
+        for d in range(3):
+            self_ref[0, :, column(lax.rem(x + d, 4), yh)] = diag[:, 128 * d : 128 * d + 128]
+        turn_out[4] = diag[:, 128:256]
+        next_copy().start()
+
+        @pl.when(yh == 0)
+        def _():
+            beside_home().wait_recv()
+            final = wide(summed[1, 0]) + wide(home_self[1])
+            place(self_ref.at[0], 1, final)
+            for xv in range(4):
+                turn_out[xv] = final[:, 128 * xv : 128 * xv + 128].astype(jnp.bfloat16)
+                turn_copy(xv).start()
+
+    def turned():
+        next_copy().wait_recv()
+        self_ref[0, :, column(lax.rem(x + 3, 4), yh)] = wide(turn_in[4]).T.astype(jnp.bfloat16)
+
+        @pl.when(yh == 1)
+        def _():
+            for xv in range(4):
+                remote(turn_in.at[xv], turn_in.at[xv], turn_s.at[xv], turn_r.at[xv], mirror).wait_recv()
+                self_ref[0, :, pl.ds(256 * xv, 128)] = wide(turn_in[xv]).T.astype(jnp.bfloat16)
+
+    diagonal()
+    compute(1, lambda i: [OWN, OWN + 1], lambda i: [OWN + 2, OWN + 3])
+    project()
     pass_on(0)
     fold(0)
     mate_copy(0).wait_recv()
@@ -365,61 +472,52 @@
     )
     fold(1)
     pass_on(1)
-    project()
-    finish(0)
+    fold(2)
     pass_on(2)
-    fold(2)
-    share_first()
     pass_on(3)
     cross_inner(0)
     piece_inner(0)
-    finish(1)
+    share_first()
+    pass_on(4)
     take_along(0)
     cross_along(0)
     piece_along(0)
-    share_second()
-    pass_on(4)
     fold(3)
     piece_cross(0)
-    score_compute()
-    finish(2)
+    fold(5)
     pass_on(5)
-    fold(5)
     fold(7)
-    score_fold()
     pass_on(6)
-    finish(3)
+    share_second()
     pass_on(7)
     cross_inner(1)
     piece_inner(1)
-    finish(5)
-    score_finish()
+    score_compute()
+    finish(0)
+    finish(1)
+    finish(2)
+    finish(3)
     take_along(1)
     cross_along(1)
     piece_along(1)
     fold(4)
+    score_fold()
     piece_cross(1)
+    finish(5)
+    fold(6)
     finish(7)
-    fold(6)
     fold(8)
+    turn()
+    score_finish()
     finish(4)
     finish(6)
     finish(8)
 
-    def place(ref, k, value):
-        for xv in range(4):
-            ref[:, pl.ds(256 * xv + 128 * k, 128)] = value[:, 128 * xv : 128 * xv + 128].astype(jnp.bfloat16)
-
-    def wide(value):
-        return value.astype(jnp.float32)
-
-    for k in range(2):
-        self_home(k).wait_recv()
-        place(self_ref.at[0], k, wide(summed[k, yh]) + wide(home_self[k]))
+    turned()
 
     @pl.when(core == 0)
     def _():
-        within_mirror().wait_recv()
+        within_mirror(0).wait_recv()
         place(cross_ref.at[0, 0], 0, wide(summed[2, yh]) + wide(home_near[0, 0]))
         remote(home_near.at[1, 1], home_near.at[1, 1], home_s.at[2, 0], near_r.at[1, 1], mate).wait_recv()
         remote(home_near.at[2, 1], home_near.at[2, 1], home_s.at[2, 0], near_r.at[2, 1], mate).wait_recv()
@@ -431,7 +529,10 @@
         for k in range(2):
             remote(box.at[0, k], box.at[0, k], home_s.at[0, 0], sems.at[0, k], mirror).wait_recv()
         for source in (1, 2):
-            remote(box.at[source], box.at[source], home_s.at[0, 0], sems.at[source, 0], mirror).wait_recv()
+            for h in range(2):
+                remote(
+                    box.at[source, h], box.at[source, h], home_s.at[0, 0], sems.at[source, h], mirror
+                ).wait_recv()
         for k in range(2):
             place(
                 out, k,
@@ -450,13 +551,20 @@
         place(score_ref, k, jnp.where(yh == 0, scores[0:4], scores[4:8]))
 
     score_home_copy().wait_send()
+    next_copy().wait_send()
+
+    @pl.when(yh == 0)
+    def _():
+        for xv in range(4):
+            turn_copy(xv).wait_send()
+
     for side in range(2):
         score_hop_copy(side).wait_send()
         score_fold_copy(side).wait_send()
     for step in range(1, 8):
         ring_copy(step).wait_send()
-    for k in range(3):
-        share_copy(k).wait_send()
+    over_copy().wait_send()
+    note_mate_copy().wait_send()
     mate_copy(0).wait_send()
 
     @pl.when(core == 0)
@@ -471,11 +579,12 @@
     for p in range(PIECES):
         for side in range(2):
             hop_copy(p, side).wait_send()
-            fold_copy(p, side).wait_send()
-        home_op(p, lambda copy: copy.wait_send())
-
-
-def gram_tiles(own, acts, grads, in_rows, out_rows, classes):
+            for h in range(2):
+                fold_copy(p, side, h).wait_send()
+            home_op(p, side, lambda copy: copy.wait_send())
+
+
+def gram_tiles(stored, acts, grads, in_rows, out_rows, classes):
     bf16 = jnp.bfloat16
     dma = pltpu.SemaphoreType.DMA
     return pl.pallas_call(
@@ -501,17 +610,21 @@
             pltpu.VMEM((2, RANK, 4096), bf16),
             pltpu.VMEM((2, RANK, 4096), bf16),
             pltpu.VMEM((16, 384), jnp.float32),
-            pltpu.VMEM((4, 8, 16, 384), bf16),
+            pltpu.VMEM((2, 8, 2, 16, 384), bf16),
             pltpu.VMEM((64, 2048), bf16),
             pltpu.VMEM((4, 2, 16, 512), bf16),
             pltpu.VMEM((2, 16, 512), bf16),
             pltpu.VMEM((2, 2, 16, 512), bf16),
             pltpu.VMEM((2, 16, 512), bf16),
             pltpu.VMEM((2, 16, 512), bf16),
-            dma((4,)), dma((7,)), dma((7,)), dma((3,)), dma((3,)),
+            pltpu.VMEM((1024, 2, 1024), bf16),
+            pltpu.VMEM((5, 128, 128), bf16),
+            pltpu.VMEM((5, 128, 128), bf16),
+            dma((5,)), dma((5,)),
+            dma((4,)), dma((7,)), dma((7,)), dma((2,)), dma((2,)),
             dma((2,)), dma((2,)), dma((2,)), dma((2,)), dma, dma,
-            dma((2,)), dma((2,)), dma((2,)), dma((8,)), dma((8,)), dma((8,)), dma((8,)), dma((2,)), dma((2,)),
-            dma((PIECES, 2)), dma((PIECES, 2)), dma((PIECES, 2)), dma((PIECES, 2)), dma((PIECES, 2)),
+            dma((8,)), dma((2,)), dma((2,)), dma((8,)), dma((8,)), dma((8,)), dma((8,)), dma((2,)), dma((2,)),
+            dma((PIECES, 2)), dma((PIECES, 2)), dma((PIECES, 2, 2)), dma((PIECES, 2, 2)), dma((PIECES, 2)),
             dma((2,)), dma((3, 2)), dma((3, 2)),
         ],
         compiler_params=pltpu.CompilerParams(
@@ -519,21 +632,35 @@
         ),
         cost_estimate=pl.CostEstimate(flops=13 * 10**9, bytes_accessed=8 * 2**20, transcendentals=0),
         name="gram_tiles",
-    )(own, acts, grads, in_rows, out_rows, classes)
+    )(stored, acts, grads, in_rows, out_rows, classes)
+
+
+def settle_kernel(*refs):
+    for src, dst in zip(refs[0:3], refs[3:6]):
+        dst[...] = src[...]
+
+
+def settle(*results):
+    return pl.pallas_call(
+        settle_kernel,
+        out_shape=tuple(jax.ShapeDtypeStruct(r.shape, r.dtype) for r in results),
+        in_specs=[pl.BlockSpec(memory_space=pltpu.VMEM)] * 3,
+        out_specs=(pl.BlockSpec(memory_space=pltpu.VMEM),) * 3,
+        name="settle",
+    )(*results)
 
 
 def per_device(activations, out_grads, in_factor, out_factor, stored_rows, example_class):
     layer_count = activations.shape[0]
     model_width = activations.shape[3]
-    chunked = stored_rows.reshape(4, 2, 128, 2, 1024).transpose(1, 3, 0, 2, 4).reshape(2, 2, 512, 1024)
-    return gram_tiles(
-        chunked,
+    return settle(*gram_tiles(
+        stored_rows,
         activations.reshape(layer_count, -1, model_width),
         out_grads.reshape(layer_count, -1, model_width),
         in_factor.transpose(0, 2, 1),
         out_factor.transpose(0, 2, 1),
         example_class,
-    )
+    ))
 
 
 def solution(mesh):

time: 131 us -> 109 us (0.83)
  Pallas kernels: 120 us -> 109 us
  local copies, waits for them, and re-layouts: 10.3 us -> 0 us
    pallas_call x1, Pallas kernels: 120 us -> 106 us  [gram_tiles(): pl.pallas_call(tiles_kernel, out_shape=(jax.ShapeDtypeStruct((1, 128, 102...]
    reshape x1 -> x0, local copies, waits for them, and re-layouts: 5.47 us -> none  [per_device(): stored_rows.reshape(4, 2, 128, 2, 1024).transpose(1, 3, 0, 2, 4)]
    unnamed x3 -> x0, local copies, waits for them, and re-layouts: 4.84 us -> none
    pallas_call x0 -> x1, Pallas kernels: none -> 2.02 us  [settle(): pl.pallas_call(settle_kernel, out_shape=tuple((jax.ShapeDtypeStruct(r.sha...]
where the time goes in v3:
time: 109 us
  Pallas kernels  109 us (100%)
    pallas_call x1, Pallas kernels, gram_tiles(): pl.pallas_call(tiles_kernel, out_shape=(jax.ShapeDtypeStruct((1, 128, 102...  106 us

profile of v3, /device:TPU:1, one launch (start us, length us, event | category | flops | bytes accessed | tf_op | source)
XLA Modules:
  0.0 109.2 jit_solution(9647469858149076992)
XLA Ops:
  0.6 106.5 %gram_tiles.1 = (bf16[1,128,1024]{2,1,0:T(8,128)(2,1)}, bf16[1,2,128,1024]{3,2,1,0:T(8,128)(2,1)}, bf16[4,1024]{1,0:T(4,128)(2,1)}) custom-call(bf16[1024,2,1024]{2,1,0:T(2,128)(2,1)} %stored_hbm.1, bf16[2,128,4096]{2,1,0:T(8,128)(2,1)} %bitcast.4, bf16[2,128,4096]{2,1,0:T(8,128)(2,1)} %bitcast.5, bf16[2,32,4096]{2,1,0:T(8,128)(2,1)} %bitcast.6, ...), custom_call_target="tpu_custom_call" | custom-call | flops 12999999488 | bytes 8388608 | tf_op jit(solution)/shard_map/gram_tiles/pallas_call | solution.py:590
  107.1 2.0 %settle.1 = (bf16[1,128,1024]{2,1,0:T(8,128)(2,1)}, bf16[1,2,128,1024]{3,2,1,0:T(8,128)(2,1)}, bf16[4,1024]{1,0:T(4,128)(2,1)}) custom-call(bf16[1,128,1024]{2,1,0:T(8,128)(2,1)} %get-tuple-element.6.refs_0_, bf16[1,2,128,1024]{3,2,1,0:T(8,128)(2,1)} %get-tuple-element.7.refs_1_, bf16[4,1024]{1,0:T(4,128)(2,1)} %get-tuple-element.8.refs_2_), custom_call_target="tpu_custom_call" | custom-call | tf_op jit(solution)/shard_map/settle/pallas_call | solution.py:644

commit v4 on v3

--- a/solution.py
+++ b/solution.py
@@ -104,8 +104,11 @@
     passes_inner = yl == core
     passed = jnp.where(passes_inner, INNER, ALONG)
 
-    def cross_copy(k):
-        return remote(chunks.at[passed + k], chunks.at[CROSS + k], cross_s.at[k], cross_r.at[k], mate)
+    def cross_copy(step):
+        k, rows = rows_of(step)
+        return remote(
+            chunks.at[passed + k, rows], chunks.at[CROSS + k, rows], cross_s.at[step], cross_r.at[step], mate
+        )
 
     def share(p, ref, h):
         if p == 0:
@@ -135,11 +138,9 @@
     def _():
         mate_copy(1).start()
 
-    def send_shares(p):
-        for side in range(2):
-            hop_copy(p, side).start()
-        for side in range(2):
-            fold_copy(p, side, 1 - side).start()
+    def send_share(p, h):
+        hop_copy(p, h).start()
+        fold_copy(p, 1 - h, h).start()
 
     def product(lefts, rights, cols):
         total = None
@@ -160,7 +161,7 @@
                             parts[0, xu, i, :, 128 * d : 128 * d + 128] = total[
                                 xu, :, 128 * (xv - 2 * n) : 128 * (xv - 2 * n) + 128
                             ]
-        send_shares(0)
+            send_share(0, i)
 
     def compute(p, left_slots, right_slots):
         for i in range(1 if p == 1 else 2):
@@ -172,7 +173,9 @@
                 return carry
 
             lax.fori_loop(0, 2, columns, 0)
-        send_shares(p)
+            send_share(p, i)
+            if p == 1:
+                send_share(p, 1)
 
     half = 1 - yl
 
@@ -284,19 +287,17 @@
         if step < 4:
             inner_copy(step + 4).start()
 
+        @pl.when(passes_inner)
+        def _():
+            cross_copy(step).start()
+
     def take_along(k):
         for step in range(4 * k, 4 * k + 4):
             along_copy(step).wait_recv()
 
-    def cross_inner(k):
-        @pl.when(passes_inner)
-        def _():
-            cross_copy(k).start()
-
-    def cross_along(k):
-        @pl.when(jnp.logical_not(passes_inner))
-        def _():
-            cross_copy(k).start()
+            @pl.when(jnp.logical_not(passes_inner))
+            def _():
+                cross_copy(step).start()
 
     def piece_inner(k):
         half_piece(3 + k, INNER + k, yl == 1)
@@ -305,7 +306,8 @@
         half_piece(5 + k, ALONG + k, yl == 0)
 
     def piece_cross(k):
-        cross_copy(k).wait_recv()
+        for step in range(4 * k, 4 * k + 4):
+            cross_copy(step).wait_recv()
         half_piece(7 + k, CROSS + k, core == 0)
 
     def over_copy():
@@ -475,12 +477,10 @@
     fold(2)
     pass_on(2)
     pass_on(3)
-    cross_inner(0)
     piece_inner(0)
     share_first()
     pass_on(4)
     take_along(0)
-    cross_along(0)
     piece_along(0)
     fold(3)
     piece_cross(0)
@@ -490,26 +490,24 @@
     pass_on(6)
     share_second()
     pass_on(7)
-    cross_inner(1)
     piece_inner(1)
     score_compute()
     finish(0)
     finish(1)
     finish(2)
+    take_along(1)
+    piece_along(1)
     finish(3)
-    take_along(1)
-    cross_along(1)
-    piece_along(1)
     fold(4)
     score_fold()
     piece_cross(1)
     finish(5)
+    finish(7)
+    finish(4)
     fold(6)
-    finish(7)
-    fold(8)
     turn()
     score_finish()
-    finish(4)
+    fold(8)
     finish(6)
     finish(8)
 
@@ -574,8 +572,8 @@
     for step in range(8):
         inner_copy(step).wait_send()
         along_copy(step).wait_send()
-    for k in range(2):
-        cross_copy(k).wait_send()
+    for step in range(8):
+        cross_copy(step).wait_send()
     for p in range(PIECES):
         for side in range(2):
             hop_copy(p, side).wait_send()
@@ -623,7 +621,7 @@
             dma((5,)), dma((5,)),
             dma((4,)), dma((7,)), dma((7,)), dma((2,)), dma((2,)),
             dma((2,)), dma((2,)), dma((2,)), dma((2,)), dma, dma,
-            dma((8,)), dma((2,)), dma((2,)), dma((8,)), dma((8,)), dma((8,)), dma((8,)), dma((2,)), dma((2,)),
+            dma((8,)), dma((2,)), dma((2,)), dma((8,)), dma((8,)), dma((8,)), dma((8,)), dma((8,)), dma((8,)),
             dma((PIECES, 2)), dma((PIECES, 2)), dma((PIECES, 2, 2)), dma((PIECES, 2, 2)), dma((PIECES, 2)),
             dma((2,)), dma((3, 2)), dma((3, 2)),
         ],

time: 109 us -> 108 us (level)
  no operation moved by 1% of the time
where the time goes in v4:
time: 108 us
  Pallas kernels  108 us (100%)
    pallas_call x1, Pallas kernels, gram_tiles(): pl.pallas_call(tiles_kernel, out_shape=(jax.ShapeDtypeStruct((1, 128, 102...  106 us

profile of v4, /device:TPU:1, one launch (start us, length us, event | category | flops | bytes accessed | tf_op | source)
XLA Modules:
  0.0 108.2 jit_solution(9634171540816358030)
XLA Ops:
  0.6 105.6 %gram_tiles.1 = (bf16[1,128,1024]{2,1,0:T(8,128)(2,1)}, bf16[1,2,128,1024]{3,2,1,0:T(8,128)(2,1)}, bf16[4,1024]{1,0:T(4,128)(2,1)}) custom-call(bf16[1024,2,1024]{2,1,0:T(2,128)(2,1)} %stored_hbm.1, bf16[2,128,4096]{2,1,0:T(8,128)(2,1)} %bitcast.4, bf16[2,128,4096]{2,1,0:T(8,128)(2,1)} %bitcast.5, bf16[2,32,4096]{2,1,0:T(8,128)(2,1)} %bitcast.6, ...), custom_call_target="tpu_custom_call" | custom-call | flops 12999999488 | bytes 8388608 | tf_op jit(solution)/shard_map/gram_tiles/pallas_call | solution.py:588
  106.2 2.0 %settle.1 = (bf16[1,128,1024]{2,1,0:T(8,128)(2,1)}, bf16[1,2,128,1024]{3,2,1,0:T(8,128)(2,1)}, bf16[4,1024]{1,0:T(4,128)(2,1)}) custom-call(bf16[1,128,1024]{2,1,0:T(8,128)(2,1)} %get-tuple-element.6.refs_0_, bf16[1,2,128,1024]{3,2,1,0:T(8,128)(2,1)} %get-tuple-element.7.refs_1_, bf16[4,1024]{1,0:T(4,128)(2,1)} %get-tuple-element.8.refs_2_), custom_call_target="tpu_custom_call" | custom-call | tf_op jit(solution)/shard_map/settle/pallas_call | solution.py:642

commit v5 on v4

--- a/solution.py
+++ b/solution.py
@@ -130,7 +130,7 @@
             fold_s.at[p, side, h], fold_r.at[p, side, h], right if side == 0 else left,
         )
 
-    for step in range(4):
+    for step in range(3):
         inner_copy(step).start()
     mate_copy(0).start()
 
@@ -284,8 +284,8 @@
     def pass_on(step):
         inner_copy(step).wait_recv()
         along_copy(step).start()
-        if step < 4:
-            inner_copy(step + 4).start()
+        if step < 5:
+            inner_copy(step + 3).start()
 
         @pl.when(passes_inner)
         def _():

time: 108 us -> 107 us (level)
  Pallas kernels: 108 us -> 106 us
    pallas_call x1, Pallas kernels: 106 us -> 104 us  [gram_tiles(): pl.pallas_call(tiles_kernel, out_shape=(jax.ShapeDtypeStruct((1, 128, 102...]
where the time goes in v5:
time: 107 us
  Pallas kernels  106 us (99%)
    pallas_call x1, Pallas kernels, gram_tiles(): pl.pallas_call(tiles_kernel, out_shape=(jax.ShapeDtypeStruct((1, 128, 102...  104 us

profile of v5, /device:TPU:1, one launch (start us, length us, event | category | flops | bytes accessed | tf_op | source)
XLA Modules:
  0.0 107.1 jit_solution(15068812086315591140)
XLA Ops:
  0.6 104.4 %gram_tiles.1 = (bf16[1,128,1024]{2,1,0:T(8,128)(2,1)}, bf16[1,2,128,1024]{3,2,1,0:T(8,128)(2,1)}, bf16[4,1024]{1,0:T(4,128)(2,1)}) custom-call(bf16[1024,2,1024]{2,1,0:T(2,128)(2,1)} %stored_hbm.1, bf16[2,128,4096]{2,1,0:T(8,128)(2,1)} %bitcast.4, bf16[2,128,4096]{2,1,0:T(8,128)(2,1)} %bitcast.5, bf16[2,32,4096]{2,1,0:T(8,128)(2,1)} %bitcast.6, ...), custom_call_target="tpu_custom_call" | custom-call | flops 12999999488 | bytes 8388608 | tf_op jit(solution)/shard_map/gram_tiles/pallas_call | solution.py:588
  105.1 2.0 %settle.1 = (bf16[1,128,1024]{2,1,0:T(8,128)(2,1)}, bf16[1,2,128,1024]{3,2,1,0:T(8,128)(2,1)}, bf16[4,1024]{1,0:T(4,128)(2,1)}) custom-call(bf16[1,128,1024]{2,1,0:T(8,128)(2,1)} %get-tuple-element.6.refs_0_, bf16[1,2,128,1024]{3,2,1,0:T(8,128)(2,1)} %get-tuple-element.7.refs_1_, bf16[4,1024]{1,0:T(4,128)(2,1)} %get-tuple-element.8.refs_2_), custom_call_target="tpu_custom_call" | custom-call | tf_op jit(solution)/shard_map/settle/pallas_call | solution.py:642
